TPU v7x, 512 devices: a whole 4x4x16 slice. The times are simulated.
512 devices in a mesh: pair: 16 (over z), section: 2 (over x_lo), shard: 16 (over x_hi, y, core).
Axes of the slice: x: 4 (x_hi: 2, x_lo: 2; x = x_hi * 2 + x_lo), y: 4, z: 16, core: 2. Of those that a mesh axis runs over, the one named last changes fastest.
Arguments:
- section_inputs: bfloat16 [2, 16384, 4096], P('section', ('pair', 'shard')), parts along dimension 1, may hold values from -72 to 72
- keys_values: bfloat16 [2, 16384, 512], P(None, ('pair', 'shard')), parts along dimension 1, may hold values from -6 to 6
- out_weight: bfloat16 [4096, 4096], P('shard', 'section'), may hold values from -0.09375 to 0.09375
Outputs:
- section_outputs: bfloat16 [2, 16384, 4096], P('section', ('pair', 'shard')), parts along dimension 1
- weight_grad: bfloat16 [65536, 4096], P(('pair', 'shard'), 'section'), parts along dimension 0
There are 16 independent parts, one for each index of `pair`. A program takes and returns all parts, laid end to end along the dimension named above; an argument that names none is the same for every part. Nothing has to cross between parts.
All inputs are finite; a program needn't handle non-finite values.
Results may differ from a plain program's by a relative error of at most 0.018.
Values may be sent and summed in bfloat16 or wider, within the bound.
A program may use at most 64 MiB of HBM per device.

v0:
```python
import math

import jax
import jax.numpy as jnp
from jax import lax
from jax.sharding import PartitionSpec as P

HEAD_DIM = 128
HEADS = 32
KV_HEADS = 4


def passed_along(value, axis, by):
    size = lax.axis_size(axis)
    pairs = [(i, i + by) for i in range(size) if 0 <= i + by < size]
    return lax.ppermute(value, axis, pairs)


def attend(queries, key_rows, value_rows):
    length = queries.shape[0]
    group_size = HEADS // KV_HEADS
    query_heads = queries.reshape(length, KV_HEADS, group_size, HEAD_DIM)
    key_heads = key_rows.reshape(length, KV_HEADS, HEAD_DIM)
    value_heads = value_rows.reshape(length, KV_HEADS, HEAD_DIM)
    scores = jnp.einsum(
        "qhgd,khd->hgqk", query_heads, key_heads, preferred_element_type=jnp.float32
    ) / math.sqrt(HEAD_DIM)
    causal = jnp.arange(length)[:, None] >= jnp.arange(length)[None, :]
    scores = jnp.where(causal, scores, -1e30)
    row_max = jnp.max(scores, axis=-1, keepdims=True)
    shifted = jnp.exp(scores - row_max)
    probs_low = (shifted / jnp.sum(shifted, axis=-1, keepdims=True)).astype(jnp.bfloat16)
    mixed = jnp.einsum("hgqk,khd->qhgd", probs_low, value_heads, preferred_element_type=jnp.float32)
    return mixed.reshape(length, HEADS * HEAD_DIM).astype(jnp.bfloat16)


def query_grad(queries, key_rows, value_rows, grad_context):
    _, pullback = jax.vjp(lambda query_part: attend(query_part, key_rows, value_rows), queries)
    return pullback(grad_context)[0]


def fold_step(cot_rows, columns, weight):
    grad_rows = lax.dot_general(
        cot_rows, weight, (((1,), (1,)), ((), ())), preferred_element_type=jnp.float32
    )
    grad_part = lax.dot_general(
        columns, cot_rows, (((0,), (0,)), ((), ())), preferred_element_type=jnp.float32
    )
    return (grad_rows, grad_part)


def body(section_inputs, keys_values, out_weight):
    second_section = lax.axis_index("section") == 1
    tok_rows = section_inputs.shape[1]
    feat_width = section_inputs.shape[2]
    half_cols = out_weight.shape[1]
    local_rows = section_inputs[0]
    key_rows = keys_values[0]
    value_rows = keys_values[1]
    context = lax.cond(
        second_section,
        lambda: jnp.zeros((tok_rows, feat_width), jnp.bfloat16),
        lambda: attend(local_rows, key_rows, value_rows),
    )
    spread = lax.all_to_all(context, "shard", split_axis=1, concat_axis=0, tiled=True)
    moved_rows = passed_along(spread, "section", 1)
    columns = jnp.where(second_section, moved_rows, spread)
    own_half = lax.psum_scatter(
        jnp.dot(columns, out_weight, preferred_element_type=jnp.float32).astype(jnp.bfloat16),
        "shard",
        scatter_dimension=0,
        tiled=True,
    )
    lower_half = passed_along(own_half, "section", 1)
    output = jnp.concatenate([lower_half, own_half], 1)
    received = passed_along(local_rows[:, :half_cols], "section", -1)
    own_cotangent = jnp.where(second_section, local_rows[:, half_cols:], received)
    partial_ctx, grad_sum = fold_step(
        lax.all_gather(own_cotangent, "shard", axis=0, tiled=True), columns, out_weight
    )
    upper_part = passed_along(partial_ctx.astype(jnp.bfloat16), "section", -1).astype(
        partial_ctx.dtype
    )
    grad_context = (partial_ctx + upper_part).astype(jnp.bfloat16)
    back_rows = lax.all_to_all(grad_context, "shard", split_axis=0, concat_axis=1, tiled=True)
    weight_grad = grad_sum.astype(jnp.bfloat16)
    grad_queries = lax.cond(
        second_section,
        lambda: jnp.zeros((tok_rows, feat_width), jnp.bfloat16),
        lambda: query_grad(local_rows, key_rows, value_rows, back_rows),
    )
    result = jnp.where(second_section, output, grad_queries)[None]
    return (result, weight_grad)


def solution(mesh):
    placed = (
        P("section", ("pair", "shard"), None),
        P(None, ("pair", "shard"), None),
        P("shard", "section"),
    )
    return jax.shard_map(
        body,
        mesh=mesh,
        in_specs=placed,
        out_specs=(P("section", ("pair", "shard"), None), P(("pair", "shard"), "section")),
        check_vma=False,
    )
```

profile of v0, /device:TPU:24, one launch (start us, length us, event | category | flops | bytes accessed | tf_op | source)
XLA Modules:
  0.0 221.0 jit_solution(3693868185841441016)
XLA Ops:
  7.2 0.0 copy-start
  7.2 0.0 all-gather.2.cloned.1.call-start
  7.2 1.0 slice.17
  8.3 1.3 collective-permute-start.2
  9.6 8.6 %collective-permute-done.2 = bf16[64,2048]{1,0:T(8,128)(2,1)S(1)} collective-permute-done((bf16[64,2048]{1,0:T(8,128)(2,1)S(1)}, bf16[64,2048]{1,0:T(8,128)(2,1)S(1)}, u32[]{:S(2)}, u32[]{:S(2)}) %collective-permute-start.2) | collective-permute-done | bytes 262176 | tf_op jit(solution)/shard_map/ppermute | solution.py:16
  18.2 1.7 slice_select_fusion
  19.9 0.0 all-gather.2.cloned.1.call-update
  19.9 0.0 reduce-scatter.2.cloned.1.call-start
  20.0 0.9 fusion.42
  20.9 3.6 %conditional.2 = (bf16[64,4096]{1,0:T(8,128)(2,1)S(1)}) conditional(s32[]{:T(128)} %convert_element_type.55, (bf16[1,64,512]{2,1,0:T(8,128)(2,1)S(1)}, bf16[1,64,4096]{2,1,0:T(8,128)(2,1)}, bf16[1,64,512]{2,1,0:T(8,128)(2,1)S(1)}) %tuple.22, () %tuple.23), branch_computations={%region_0.3_spmd, %region_3.4_spmd} | conditional | flops 102111360 | bytes 6254600 | solution.py:60
  20.9 1.1 copy.73
  22.1 0.8 fusion.37
  22.8 0.6 fusion.4
  23.5 0.4 fusion.5
  23.9 0.3 copy.47
  24.3 0.2 copy.116
  24.6 17.2 %all_to_all.39 = bf16[64,16,256]{2,0,1:T(8,128)(2,1)S(1)} all-to-all(bf16[64,16,256]{2,0,1:T(8,128)(2,1)S(1)} %bitcast.107), channel_id=1, replica_groups=mesh['pair'=16,'section'=2,'shard'=16] {'shard'}, dimensions={1} | all-to-all | bytes 1048576 | tf_op jit(solution)/shard_map/all_to_all | solution.py:65
  41.7 1.3 collective-permute-start
  43.1 13.6 %collective-permute-done = bf16[1024,256]{1,0:T(8,128)(2,1)S(1)} collective-permute-done((bf16[1024,256]{1,0:T(8,128)(2,1)S(1)}, bf16[1024,256]{1,0:T(8,128)(2,1)S(1)}, u32[]{:S(2)}, u32[]{:S(2)}) %collective-permute-start) | collective-permute-done | bytes 524320 | tf_op jit(solution)/shard_map/ppermute | solution.py:16
  56.7 0.0 copy-done
  56.7 3.2 %convolution_convert_fusion.3 = bf16[1024,2048]{1,0:T(8,128)(2,1)} fusion(bf16[256,2048]{1,0:T(8,128)(2,1)S(1)} %copy-done, bf16[1024,256]{1,0:T(8,128)(2,1)S(1)} %collective-permute-done, bf16[1024,256]{1,0:T(8,128)(2,1)S(1)} %bitcast.97, pred[]{:T(512)S(6)} %eq.12), kind=kOutput, calls=%fused_computation.52 | convolution fusion | flops 1076101120 | bytes 6291457 | tf_op jit(solution)/shard_map/dot_general | solution.py:69
  59.9 0.0 reduce-scatter.2.cloned.1.call-update
  59.9 34.0 %all-gather.2.cloned.1.call-done = bf16[1024,2048]{1,0:T(8,128)(2,1)} async-done(((bf16[64,2048]{1,0:T(8,128)(2,1)}), bf16[1024,2048]{1,0:T(8,128)(2,1)}) %all-gather.2.cloned.1.call-update) | async-done | bytes 4194320 | tf_op jit(solution)/shard_map/all_gather | solution.py:79
  94.0 3.5 %fusion.43 = (bf16[1024,256]{1,0:T(8,128)(2,1)S(1)}, f32[1024,256]{1,0:T(8,128)S(1)}) fusion(bf16[1024,2048]{1,0:T(8,128)(2,1)} %all-gather.2.cloned.1.call-done, bf16[256,2048]{1,0:T(8,128)(2,1)S(1)} %copy-done), kind=kOutput, calls=%fused_computation.62 | convolution fusion | flops 1074003968 | bytes 6815744 | tf_op jit(solution)/shard_map/dot_general | solution.py:43
  97.5 1.3 collective-permute-start.3
  98.8 14.7 %collective-permute-done.3 = bf16[1024,256]{1,0:T(8,128)(2,1)S(1)} collective-permute-done((bf16[1024,256]{1,0:T(8,128)(2,1)S(1)}, bf16[1024,256]{1,0:T(8,128)(2,1)S(1)}, u32[]{:S(2)}, u32[]{:S(2)}) %collective-permute-start.3) | collective-permute-done | bytes 524320 | tf_op jit(solution)/shard_map/ppermute | solution.py:16
  113.4 1.0 add_convert_fusion
  114.4 5.6 %all-to-all-start.1 = ((bf16[16,64,256]{2,1,0:T(8,128)(2,1)}), bf16[16,64,256]{2,1,0:T(8,128)(2,1)S(1)}, u32[]{:S(2)}, u32[]{:S(2)}) async-start(bf16[16,64,256]{2,1,0:T(8,128)(2,1)} %bitcast.18), calls=%async_computation.2 | async-start | bytes 1048576 | tf_op jit(solution)/shard_map/all_to_all | solution.py:85
  120.1 81.7 %reduce-scatter.2.cloned.1.call-done = bf16[64,2048]{1,0:T(8,128)(2,1)} async-done(((bf16[1024,2048]{1,0:T(8,128)(2,1)}), bf16[64,2048]{1,0:T(8,128)(2,1)}) %reduce-scatter.2.cloned.1.call-update) | async-done | bytes 262160 | tf_op jit(solution)/shard_map/reduce_scatter | solution.py:68
  201.8 2.5 %collective-permute-start.1 = (bf16[64,2048]{1,0:T(8,128)(2,1)}, bf16[64,2048]{1,0:T(8,128)(2,1)S(1)}, u32[]{:S(2)}, u32[]{:S(2)}) collective-permute-start(bf16[64,2048]{1,0:T(8,128)(2,1)} %reduce-scatter.2.cloned.1.call-done), channel_id=1, source_target_pairs={{0,16},{1,17},{2,18},{3,19},{4,20},{5,21},{6,22},{7,23},{8,24},{9,... | collective-permute-start | bytes 786440 | tf_op jit(solution)/shard_map/ppermute | solution.py:16
  204.3 4.4 %convolution_convert_fusion.4 = bf16[256,2048]{1,0:T(8,128)(2,1)} fusion(bf16[1024,2048]{1,0:T(8,128)(2,1)} %all-gather.2.cloned.1.call-done, bf16[1024,256]{1,0:T(8,128)(2,1)S(1)} %collective-permute-done, bf16[1024,256]{1,0:T(8,128)(2,1)S(1)} %bitcast.98, pred[]{:T(512)S(6)} %eq.12), kind=kOutput, calls=%fused_computation.53 | convolution fusion | flops 1074528256 | bytes 6291457 | tf_op jit(solution)/shard_map/dot_general | solution.py:46
  208.7 0.0 all-to-all-done.1
  208.7 0.0 copy-done.1
  208.7 4.5 %conditional.3 = (bf16[64,4096]{1,0:T(8,128)(2,1)S(1)}) conditional(s32[]{:T(128)} %convert_element_type.55, (bf16[64,16,256]{2,0,1:T(8,128)(2,1)S(1)}, bf16[1,64,512]{2,1,0:T(8,128)(2,1)S(1)}, bf16[1,64,512]{2,1,0:T(8,128)(2,1)S(1)}, bf16[1,64,4096]{2,1,0:T(8,128)(2,1)S(1)}) %tuple.43, () %tuple.25), branch_computations={%region_5.11_spmd, %region_11.12_spmd} | conditional | flops 105259008 | bytes 11948040 | solution.py:87
  208.8 0.1 copy.75
  208.9 0.3 copy.56
  209.2 0.2 reshape.34
  209.4 0.6 fusion.28
  210.1 0.2 fusion.29
  210.3 0.7 fusion.24
  211.1 0.6 fusion.27
  211.7 0.5 fusion.22
  212.3 0.3 copy.52
  212.6 0.3 fusion.16
  212.9 0.1 copy.54
  213.0 0.2 copy.115
  213.2 0.0 collective-permute-done.1
  213.2 0.9 fusion.36
  (14 shorter events, 0.2 us)
Async XLA Ops:
  7.2 49.5 %copy-start = (bf16[256,2048]{1,0:T(8,128)(2,1)S(1)}, bf16[256,2048]{1,0:T(8,128)(2,1)}, u32[]{:S(2)}) copy-start(bf16[256,2048]{1,0:T(8,128)(2,1)} %param.9) | copy-start | bytes 3145732
  7.2 86.8 %all-gather.2.cloned.1.call-start = ((), (), s32[]{:S(2)}) async-start(), calls=%async_computation.4 | async-start | bytes 4456448 | tf_op jit(solution)/shard_map/all_gather | solution.py:79
  8.3 9.9 %collective-permute-start.2 = (bf16[64,2048]{1,0:T(8,128)(2,1)S(1)}, bf16[64,2048]{1,0:T(8,128)(2,1)S(1)}, u32[]{:S(2)}, u32[]{:S(2)}) collective-permute-start(bf16[64,2048]{1,0:T(8,128)(2,1)S(1)} %slice.17), channel_id=1, source_target_pairs={{16,0},{17,1},{18,2},{19,3},{20,4},{21,5},{22,6},{23,7},{24,8},{25... | collective-permute-start | bytes 786440 | tf_op jit(solution)/shard_map/ppermute | solution.py:16
  19.9 181.9 %reduce-scatter.2.cloned.1.call-start = ((), (), s32[]{:S(2)}) async-start(), calls=%async_computation.3 | async-start | bytes 4456448 | tf_op jit(solution)/shard_map/reduce_scatter | solution.py:68
  41.7 14.9 %collective-permute-start = (bf16[1024,256]{1,0:T(8,128)(2,1)S(1)}, bf16[1024,256]{1,0:T(8,128)(2,1)S(1)}, u32[]{:S(2)}, u32[]{:S(2)}) collective-permute-start(bf16[1024,256]{1,0:T(8,128)(2,1)S(1)} %bitcast.96), channel_id=1, source_target_pairs={{0,16},{1,17},{2,18},{3,19},{4,20},{5,21},{6,22},{7,23},{8,24},{9,... | collective-permute-start | bytes 1572872 | tf_op jit(solution)/shard_map/ppermute | solution.py:16
  97.5 16.0 %collective-permute-start.3 = (bf16[1024,256]{1,0:T(8,128)(2,1)S(1)}, bf16[1024,256]{1,0:T(8,128)(2,1)S(1)}, u32[]{:S(2)}, u32[]{:S(2)}) collective-permute-start(bf16[1024,256]{1,0:T(8,128)(2,1)S(1)} %get-tuple-element.44), channel_id=1, source_target_pairs={{16,0},{17,1},{18,2},{19,3},{20,4},{21,5},{22,6},{23,7},{24,8},{25... | collective-permute-start | bytes 1572872 | tf_op jit(solution)/shard_map/ppermute | solution.py:16
  114.4 94.3 %copy-start.1 = (bf16[1,64,4096]{2,1,0:T(8,128)(2,1)S(1)}, bf16[1,64,4096]{2,1,0:T(8,128)(2,1)}, u32[]{:S(2)}) copy-start(bf16[1,64,4096]{2,1,0:T(8,128)(2,1)} %param.7) | copy-start | bytes 1572868
  114.4 94.3 %all-to-all-start.1 = ((bf16[16,64,256]{2,1,0:T(8,128)(2,1)}), bf16[16,64,256]{2,1,0:T(8,128)(2,1)S(1)}, u32[]{:S(2)}, u32[]{:S(2)}) async-start(bf16[16,64,256]{2,1,0:T(8,128)(2,1)} %bitcast.18), calls=%async_computation.2 | async-start | bytes 1048576 | tf_op jit(solution)/shard_map/all_to_all | solution.py:85
  201.8 11.4 %collective-permute-start.1 = (bf16[64,2048]{1,0:T(8,128)(2,1)}, bf16[64,2048]{1,0:T(8,128)(2,1)S(1)}, u32[]{:S(2)}, u32[]{:S(2)}) collective-permute-start(bf16[64,2048]{1,0:T(8,128)(2,1)} %reduce-scatter.2.cloned.1.call-done), channel_id=1, source_target_pairs={{0,16},{1,17},{2,18},{3,19},{4,20},{5,21},{6,22},{7,23},{8,24},{9,... | collective-permute-start | bytes 786440 | tf_op jit(solution)/shard_map/ppermute | solution.py:16
  208.7 4.5 %copy-start.2 = (bf16[64,2048]{1,0:T(8,128)(2,1)S(1)}, bf16[64,2048]{1,0:T(8,128)(2,1)}, u32[]{:S(2)}) copy-start(bf16[64,2048]{1,0:T(8,128)(2,1)} %reduce-scatter.2.cloned.1.call-done) | copy-start | bytes 786436
Sparse Core Ops, SparseCore 0:
  20.0 73.8 all-gather.1
  98.8 102.9 reduce-scatter.1
where the time goes:
time: 222 us; the launch traced here: 221 us
  waiting for transfers between devices  153 us (69%)
  blocking collectives  17.2 us (8%)
  matrix products  14.6 us (7%)
  between operations  14.1 us (6%)
  starting transfers between devices  12.1 us (5%)
  other arithmetic  5.06 us (2%)
  local copies, waits for them, and re-layouts  4.96 us (2%)
    reduce_scatter x1, waiting for transfers between devices, body(): lax.psum_scatter(jnp.dot(columns, out_weight, preferred_element_type=jnp....  81.7 us
    ppermute x4, waiting for transfers between devices, passed_along(): return lax.ppermute(value, axis, pairs)  36.9 us
    all_gather x1, waiting for transfers between devices, body(): lax.all_gather(own_cotangent, 'shard', axis=0, tiled=True)  34 us
    all_to_all x1, blocking collectives, body(): lax.all_to_all(context, 'shard', split_axis=1, concat_axis=0, tiled=True)  17.2 us
    ppermute x4, starting transfers between devices, passed_along(): return lax.ppermute(value, axis, pairs)  6.37 us
    all_to_all x1, starting transfers between devices, body(): lax.all_to_all(grad_context, 'shard', split_axis=0, concat_axis=1, tiled=...  5.65 us
  transfers between devices with their start and end apart: 7, of which 5 were waited for; matrix products, arithmetic and copies ran while one was open for 9% of the time, Pallas kernels for 0%

commit v1 on v0

v1 whole, which is shorter than its diff:
```python
import functools
import math

import jax
import jax.numpy as jnp
from jax import lax
from jax.experimental import pallas as pl
from jax.experimental.pallas import tpu as pltpu
from jax.sharding import PartitionSpec as P

HEAD_DIM = 128
GROUP = 8
KV_HEADS = 4
TOK = 64
FEAT = 256
HALF = 2048
N_TILE = 512
SCALE = 1.0 / math.sqrt(HEAD_DIM)
BF16 = jnp.bfloat16
F32 = jnp.float32
NT = (((1,), (1,)), ((), ()))


def place_of_head(head):
    shard = head // 2
    return (shard // 2) % 4, (shard // 8) * 2 + shard % 2, (head % 2) * HEAD_DIM


def kernel(
    x_ref, kv_ref, w_ref, out_ref, dw_ref,
    q_v, kv_v, w_v, probs, cs, c1, cg, ct, g, op, ra, fwd, bwd, xr, dp, dr, ds, dc, res, dw_v,
    send_sem, load_sem, g_sem, c1_sem, cg_sem, ra_sem, f_sem, b_sem, xr_sem, dr_sem, dc_sem,
):
    s = lax.axis_index("section")
    shard = lax.axis_index("shard")
    c = lax.rem(shard, 2)
    y = lax.rem(shard // 2, 4)
    xh = shard // 8
    oc, ox, osec = 1 - c, 1 - xh, 1 - s
    yp, y2, ym = lax.rem(y + 1, 4), lax.rem(y + 2, 4), lax.rem(y + 3, 4)
    first, second = s == 0, s == 1
    k_me = xh * 2 + c

    def at(xh_, y_, c_, s_):
        return {"section": s_, "shard": (xh_ * 4 + y_) * 2 + c_}

    sibling = at(xh, y, oc, s)
    up, across, down = at(xh, yp, c, s), at(xh, y2, c, s), at(xh, ym, c, s)
    row = [(dx, d_c, d_s) for d_s in (0, 1) for dx in (0, 1) for d_c in (0, 1)]
    near = {}
    for dx, d_c, d_s in row:
        near[dx, d_c, d_s] = at(ox if dx else xh, y, oc if d_c else c, d_s)
    k_at = {(dx, d_c): (ox if dx else xh) * 2 + (oc if d_c else c) for dx in (0, 1) for d_c in (0, 1)}
    columns_of = [at(a, y, c, 1) for a in (0, 1)]
    sent = {None: [], 0: [], 1: []}
    count = [0]

    def send(when, src, dst, sem, to):
        slot = count[0]
        count[0] += 1

        def copy():
            return pltpu.make_async_remote_copy(
                src_ref=src(), dst_ref=dst(), send_sem=send_sem.at[slot], recv_sem=sem(),
                device_id=to, device_id_type=pl.DeviceIdType.MESH)

        copy().start()
        sent[when].append(copy)

    def arrive(dst, sem):
        pltpu.make_async_remote_copy(
            src_ref=dst, dst_ref=dst, send_sem=send_sem.at[0], recv_sem=sem,
            device_id=sibling, device_id_type=pl.DeviceIdType.MESH).wait_recv()

    def k_own(a):
        return a * 2 + c

    def k_other(a):
        return a * 2 + oc

    def load(src, dst, i):
        return pltpu.make_async_copy(src, dst, load_sem.at[i])

    load_w = lambda: load(w_ref, w_v, 0)
    load_q = lambda: load(x_ref.at[0], q_v, 1)
    load_kv = lambda: load(kv_ref, kv_v, 2)
    load_own = lambda: load(x_ref.at[0, :, pl.ds(HALF, HALF)], g.at[k_me, y], 3)
    load_w().start()

    @pl.when(first)
    def _():
        load_kv().start()
        load_q().start()

    @pl.when(second)
    def _():
        load_own().start()

    barrier = pltpu.get_barrier_semaphore()
    for dx, d_c, d_s in row[1:]:
        pl.semaphore_signal(barrier, inc=1, device_id=at(ox if dx else xh, y, oc if d_c else c, osec if d_s else s),
                            device_id_type=pl.DeviceIdType.MESH)
    for other in (up, across, down):
        pl.semaphore_signal(barrier, inc=1, device_id=other, device_id_type=pl.DeviceIdType.MESH)
    pl.semaphore_wait(barrier, 10)

    def chunk(k, y_):
        return lambda: g.at[k, y_]

    def chunk_sem(k, y_):
        return lambda: g_sem.at[k, y_]

    def spread(when, k, src):
        send(when, src, chunk(k, y), chunk_sem(k, y), up)
        send(when, src, chunk(k, y), chunk_sem(k, y), down)
        send(when, src, chunk(k, y), chunk_sem(k, y), sibling)

    @pl.when(second)
    def _():
        low = lambda: x_ref.at[0, :, pl.ds(0, HALF)]
        high = lambda: x_ref.at[0, :, pl.ds(HALF, HALF)]
        send(1, low, chunk(k_me, y), chunk_sem(k_me, y), near[0, 0, 0])
        send(1, low, chunk(k_me, y), chunk_sem(k_me, y), near[1, 0, 0])
        send(1, high, chunk(k_me, y), chunk_sem(k_me, y), near[1, 0, 1])
        spread(1, k_me, high)

    @pl.when(first)
    def _():
        load_kv().wait()
        load_q().wait()
        causal = (lax.rem(lax.broadcasted_iota(jnp.int32, (GROUP * TOK, TOK), 0), TOK)
                  >= lax.broadcasted_iota(jnp.int32, (GROUP * TOK, TOK), 1))
        for h in (0, 2, 1, 3):
            keys = kv_v[0, :, h * HEAD_DIM:(h + 1) * HEAD_DIM]
            values = kv_v[1, :, h * HEAD_DIM:(h + 1) * HEAD_DIM]
            heads = [h * GROUP + i for i in range(GROUP)]
            queries = jnp.concatenate([q_v[:, i * HEAD_DIM:(i + 1) * HEAD_DIM] for i in heads], axis=0)
            scores = lax.dot_general(queries, keys, NT, preferred_element_type=F32) * SCALE
            scores = jnp.where(causal, scores, -1e30)
            shifted = jnp.exp(scores - jnp.max(scores, axis=-1, keepdims=True))
            weights = shifted * (1.0 / jnp.sum(shifted, axis=-1, keepdims=True))
            probs[h] = weights
            mixed = jnp.dot(weights.astype(BF16), values, preferred_element_type=F32).astype(BF16)
            for i, head in enumerate(heads):
                y_, k_, col = place_of_head(head)
                cs[y_, k_, :, col:col + HEAD_DIM] = mixed[i * TOK:(i + 1) * TOK]
        for y_, to in ((y2, across), (yp, up), (ym, down)):
            send(0, lambda y_=y_: cs.at[y_], lambda: c1.at[:, y], lambda: c1_sem.at[y], to)
        c1[:, y] = cs[y]

    @pl.when(first)
    def _():
        arrive(g.at[k_me, y], g_sem.at[k_me, y])
        spread(0, k_me, chunk(k_me, y))

    k_ox = ox * 2 + c
    arrive(g.at[k_ox, y], g_sem.at[k_ox, y])
    spread(None, k_ox, chunk(k_ox, y))

    @pl.when(first)
    def _():
        for y_ in (yp, ym, y2):
            arrive(c1.at[:, y_], c1_sem.at[y_])
        for dx, d_c, d_s in row[1:]:
            k_ = k_at[dx, d_c]
            send(0, lambda k_=k_: c1.at[k_], lambda: cg.at[k_me], lambda: cg_sem.at[k_me], near[dx, d_c, d_s])
        cg[k_me] = c1[k_me]

    def relay(k, y_, to):
        arrive(g.at[k, y_], g_sem.at[k, y_])
        if to is not None:
            send(None, chunk(k, y_), chunk(k, y_), chunk_sem(k, y_), to)
        send(None, chunk(k, y_), chunk(k, y_), chunk_sem(k, y_), sibling)

    relay(k_own(0), ym, up)
    relay(k_own(1), yp, down)

    load_w().wait()

    @pl.when(first)
    def _():
        for a, k in ((0, k_other(0)), (1, k_other(1)), (ox, k_own(ox))):
            arrive(cg.at[k], cg_sem.at[k])

    @pl.when(second)
    def _():
        for k in range(4):
            arrive(cg.at[k], cg_sem.at[k])

    def partial(k):
        block = cg[k].reshape(4 * TOK, FEAT)

        @pl.loop(0, HALF // N_TILE)
        def _(n):
            cols = pl.ds(pl.multiple_of(n * N_TILE, N_TILE), N_TILE)
            value = jnp.dot(block, w_v[:, cols], preferred_element_type=F32).astype(BF16)
            op[k, :, :, cols] = value.reshape(4, TOK, N_TILE)

    for a in (0, 1):
        partial(k_other(a))
        for y_ in (y2, yp, ym, y):
            send(None, lambda a=a, y_=y_: op.at[k_other(a), y_], lambda a=a, y_=y_: ra.at[a, y_],
                 lambda a=a, y_=y_: ra_sem.at[a, y_], sibling)
    for a in (0, 1):
        partial(k_own(a))

    def total(a, y_, extra):
        arrive(ra.at[a, y_], ra_sem.at[a, y_])
        k = k_own(a)

        @pl.loop(0, HALF // N_TILE)
        def _(n):
            cols = pl.ds(pl.multiple_of(n * N_TILE, N_TILE), N_TILE)
            value = op[k, y_, :, cols].astype(F32) + ra[a, y_, :, cols].astype(F32)
            for ref, i in extra:
                value += ref[i, :, cols].astype(F32)
            op[k, y_, :, cols] = value.astype(BF16)

    def pass_on(a, y_, buffer, sems, i, to):
        send(None, lambda: op.at[k_own(a), y_], lambda: buffer.at[i], lambda: sems.at[i], to)

    total(0, y2, [])
    pass_on(0, y2, fwd, f_sem, 0, up)
    total(1, y2, [])
    pass_on(1, y2, bwd, b_sem, 0, down)
    total(1, yp, [])
    pass_on(1, yp, fwd, f_sem, 1, up)
    total(0, ym, [])
    pass_on(0, ym, bwd, b_sem, 1, down)

    relay(k_own(1), ym, None)
    relay(k_own(0), yp, None)
    relay(k_own(0), y2, None)
    relay(k_own(1), y2, None)

    arrive(fwd.at[0], f_sem.at[0])
    total(0, yp, [(fwd, 0)])
    pass_on(0, yp, fwd, f_sem, 2, up)
    arrive(bwd.at[0], b_sem.at[0])
    total(1, ym, [(bwd, 0)])
    pass_on(1, ym, bwd, b_sem, 2, down)

    @pl.when(second)
    def _():
        load_own().wait()

    for k in (k_other(0), k_other(1)):
        for y_ in range(4):
            arrive(g.at[k, y_], g_sem.at[k, y_])

    def grad(k):
        block = g[k].reshape(4 * TOK, HALF)
        value = lax.dot_general(block, w_v[...], NT, preferred_element_type=F32)
        dp[k] = value.astype(BF16).reshape(4, TOK, FEAT)

    for dx, d_c in ((1, 1), (0, 1), (1, 0), (0, 0)):
        k_ = k_at[dx, d_c]
        grad(k_)
        src = lambda k_=k_: dp.at[k_]
        dst = lambda: dr.at[s, k_me]
        sem = lambda: dr_sem.at[s, k_me]
        if dx == 0 and d_c == 0:
            @pl.when(second)
            def _():
                send(1, src, dst, sem, near[0, 0, 0])

            @pl.when(first)
            def _():
                dr[0, k_me] = dp[k_me]
        else:
            send(None, src, dst, sem, near[dx, d_c, 0])

    ct[...] = cg[...].reshape(16 * TOK, FEAT).T

    @pl.loop(0, HALF // FEAT)
    def _(n):
        cols = pl.ds(pl.multiple_of(n * FEAT, FEAT), FEAT)
        block = g[:, :, :, cols].reshape(16 * TOK, FEAT)
        dw_v[:, cols] = jnp.dot(ct[...], block, preferred_element_type=F32).astype(BF16)

    store_dw = lambda: load(dw_v, dw_ref, 4)
    store_dw().start()

    @pl.when(first)
    def _():
        for s_ in (0, 1):
            for dx, d_c in ((1, 1), (0, 1), (1, 0), (0, 0)):
                if s_ or dx or d_c:
                    k_ = k_at[dx, d_c]
                    arrive(dr.at[s_, k_], dr_sem.at[s_, k_])
        for k in range(4):
            ds[:, k] = (dr[0, k].astype(F32) + dr[1, k].astype(F32)).astype(BF16)
        for y_, to in ((y2, across), (yp, up), (ym, down)):
            send(0, lambda y_=y_: ds.at[y_], lambda: dc.at[y], lambda: dc_sem.at[y], to)
        dc[y] = ds[y]

    for i in (1, 2):
        arrive(fwd.at[i], f_sem.at[i])
        arrive(bwd.at[i], b_sem.at[i])
    total(0, y, [(fwd, 2), (bwd, 1)])
    total(1, y, [(fwd, 1), (bwd, 2)])

    @pl.when(first)
    def _():
        for a in (0, 1):
            send(0, lambda a=a: op.at[k_own(a), y], lambda: xr.at[xh], lambda: xr_sem.at[xh], columns_of[a])

    @pl.when(second)
    def _():
        send(1, lambda: op.at[k_ox, y], lambda: xr.at[2], lambda: xr_sem.at[2], near[1, 0, 1])

    @pl.when(first)
    def _():
        for y_ in (yp, ym, y2):
            arrive(dc.at[y_], dc_sem.at[y_])
        for h in range(KV_HEADS):
            keys = kv_v[0, :, h * HEAD_DIM:(h + 1) * HEAD_DIM]
            values = kv_v[1, :, h * HEAD_DIM:(h + 1) * HEAD_DIM]
            heads = [h * GROUP + i for i in range(GROUP)]
            parts = []
            for head in heads:
                y_, k_, col = place_of_head(head)
                parts.append(dc[y_, k_, :, col:col + HEAD_DIM])
            grads = jnp.concatenate(parts, axis=0)
            grad_probs = lax.dot_general(grads, values, NT, preferred_element_type=F32)
            weights = probs[h]
            mean = jnp.sum(weights * grad_probs, axis=-1, keepdims=True)
            grad_scores = (weights * (grad_probs - mean) * SCALE).astype(BF16)
            grad_queries = jnp.dot(grad_scores, keys, preferred_element_type=F32).astype(BF16)
            for i, head in enumerate(heads):
                res[:, head * HEAD_DIM:(head + 1) * HEAD_DIM] = grad_queries[i * TOK:(i + 1) * TOK]

    @pl.when(second)
    def _():
        for i in range(3):
            arrive(xr.at[i], xr_sem.at[i])

        @pl.loop(0, HALF // N_TILE)
        def _(n):
            cols = pl.ds(pl.multiple_of(n * N_TILE, N_TILE), N_TILE)
            high = pl.ds(pl.multiple_of(HALF + n * N_TILE, N_TILE), N_TILE)
            res[:, cols] = (xr[0, :, cols].astype(F32) + xr[1, :, cols].astype(F32)).astype(BF16)
            res[:, high] = (xr[2, :, cols].astype(F32) + op[k_me, y, :, cols].astype(F32)).astype(BF16)

    store_res = lambda: load(res, out_ref.at[0], 5)
    store_res().start()

    for copy in sent[None]:
        copy().wait_send()
    for which in (0, 1):
        @pl.when(s == which)
        def _():
            for copy in sent[which]:
                copy().wait_send()
    store_dw().wait()
    store_res().wait()


def body(section_inputs, keys_values, out_weight):
    dma = pltpu.SemaphoreType.DMA
    scratch = [
        pltpu.VMEM((TOK, 4096), BF16),
        pltpu.VMEM((2, TOK, 512), BF16),
        pltpu.VMEM((FEAT, HALF), BF16),
        pltpu.VMEM((KV_HEADS, GROUP * TOK, TOK), F32),
        pltpu.VMEM((4, 4, TOK, FEAT), BF16),
        pltpu.VMEM((4, 4, TOK, FEAT), BF16),
        pltpu.VMEM((4, 4, TOK, FEAT), BF16),
        pltpu.VMEM((FEAT, 16 * TOK), BF16),
        pltpu.VMEM((4, 4, TOK, HALF), BF16),
        pltpu.VMEM((4, 4, TOK, HALF), BF16),
        pltpu.VMEM((2, 4, TOK, HALF), BF16),
        pltpu.VMEM((3, TOK, HALF), BF16),
        pltpu.VMEM((3, TOK, HALF), BF16),
        pltpu.VMEM((3, TOK, HALF), BF16),
        pltpu.VMEM((4, 4, TOK, FEAT), BF16),
        pltpu.VMEM((2, 4, 4, TOK, FEAT), BF16),
        pltpu.VMEM((4, 4, TOK, FEAT), BF16),
        pltpu.VMEM((4, 4, TOK, FEAT), BF16),
        pltpu.VMEM((TOK, 4096), BF16),
        pltpu.VMEM((FEAT, HALF), BF16),
        dma((64,)), dma((6,)), dma((4, 4)), dma((4,)), dma((4,)), dma((2, 4)), dma((3,)), dma((3,)), dma((3,)),
        dma((2, 4)), dma((4,)),
    ]
    anywhere = pl.BlockSpec(memory_space=pl.ANY)
    return pl.pallas_call(
        kernel,
        out_shape=(jax.ShapeDtypeStruct(section_inputs.shape, BF16), jax.ShapeDtypeStruct(out_weight.shape, BF16)),
        in_specs=[anywhere] * 3,
        out_specs=(anywhere, anywhere),
        scratch_shapes=scratch,
        compiler_params=pltpu.CompilerParams(
            collective_id=0, has_side_effects=True, vmem_limit_bytes=48 * 1024 * 1024),
        cost_estimate=pl.CostEstimate(flops=3 * 2 * 1024 * 256 * 2048, bytes_accessed=4 << 20, transcendentals=1 << 17),
    )(section_inputs, keys_values, out_weight)


def solution(mesh):
    placed = (
        P("section", ("pair", "shard"), None),
        P(None, ("pair", "shard"), None),
        P("shard", "section"),
    )
    return jax.shard_map(
        body,
        mesh=mesh,
        in_specs=placed,
        out_specs=(P("section", ("pair", "shard"), None), P(("pair", "shard"), "section")),
        check_vma=False,
    )
```

time: 222 us -> 72.5 us (0.33)
  the two profiles are of different devices: /device:TPU:24 before, /device:TPU:23 now
where the time goes in v1:
time: 72.5 us; the launch traced here: 72.3 us
  Pallas kernels  66.7 us (92%)
  local copies, waits for them, and re-layouts  4.93 us (7%)
    pallas_call x1, Pallas kernels, body(): pl.pallas_call(kernel, out_shape=(jax.ShapeDtypeStruct(section_inputs.sha...  66.7 us
    unnamed x8, local copies, waits for them, and re-layouts  4.93 us

profile of v1, /device:TPU:23, one launch (start us, length us, event | category | flops | bytes accessed | tf_op | source)
XLA Modules:
  0.0 72.3 jit_solution(1742008734310286082)
XLA Ops:
  0.6 0.0 copy-start
  0.6 1.2 %copy-done = bf16[256,2048]{1,0:T(8,128)(2,1)S(1)} copy-done((bf16[256,2048]{1,0:T(8,128)(2,1)S(1)}, bf16[256,2048]{1,0:T(8,128)(2,1)}, u32[]{:S(2)}) %copy-start) | copy-done | bytes 1048600
  1.9 0.0 copy-start.1
  1.9 1.0 %copy-done.1 = bf16[1,64,4096]{2,1,0:T(8,128)(2,1)S(1)} copy-done((bf16[1,64,4096]{2,1,0:T(8,128)(2,1)S(1)}, bf16[1,64,4096]{2,1,0:T(8,128)(2,1)}, u32[]{:S(2)}) %copy-start.1) | copy-done | bytes 524312
  2.9 0.0 copy-start.2
  2.9 0.9 %copy-done.2 = bf16[2,64,512]{2,1,0:T(8,128)(2,1)S(1)} copy-done((bf16[2,64,512]{2,1,0:T(8,128)(2,1)S(1)}, bf16[2,64,512]{2,1,0:T(8,128)(2,1)}, u32[]{:S(2)}) %copy-start.2) | copy-done | bytes 131096
  3.8 66.7 %shard_map.50 = (bf16[1,64,4096]{2,1,0:T(8,128)(2,1)S(1)}, bf16[256,2048]{1,0:T(8,128)(2,1)S(1)}) custom-call(bf16[1,64,4096]{2,1,0:T(8,128)(2,1)S(1)} %copy-done.1, bf16[2,64,512]{2,1,0:T(8,128)(2,1)S(1)} %copy-done.2, bf16[256,2048]{1,0:T(8,128)(2,1)S(1)} %copy-done), custom_call_target="tpu_custom_call" | custom-call | flops 3221225472 | bytes 4194304 | tf_op jit(solution)/shard_map/pallas_call | solution.py:386
  70.6 0.8 %copy.7 = bf16[1,64,4096]{2,1,0:T(8,128)(2,1)} copy(bf16[1,64,4096]{2,1,0:T(8,128)(2,1)S(1)} %get-tuple-element.4) | data formatting | bytes 1048576
  71.4 1.0 %copy.8 = bf16[256,2048]{1,0:T(8,128)(2,1)} copy(bf16[256,2048]{1,0:T(8,128)(2,1)S(1)} %get-tuple-element.5) | data formatting | bytes 2097152
Async XLA Ops:
  0.6 1.2 %copy-start = (bf16[256,2048]{1,0:T(8,128)(2,1)S(1)}, bf16[256,2048]{1,0:T(8,128)(2,1)}, u32[]{:S(2)}) copy-start(bf16[256,2048]{1,0:T(8,128)(2,1)} %w_ref.1) | copy-start | bytes 3145732
  1.9 1.0 %copy-start.1 = (bf16[1,64,4096]{2,1,0:T(8,128)(2,1)S(1)}, bf16[1,64,4096]{2,1,0:T(8,128)(2,1)}, u32[]{:S(2)}) copy-start(bf16[1,64,4096]{2,1,0:T(8,128)(2,1)} %x_ref.1) | copy-start | bytes 1572868
  2.9 0.9 %copy-start.2 = (bf16[2,64,512]{2,1,0:T(8,128)(2,1)S(1)}, bf16[2,64,512]{2,1,0:T(8,128)(2,1)}, u32[]{:S(2)}) copy-start(bf16[2,64,512]{2,1,0:T(8,128)(2,1)} %kv_ref.1) | copy-start | bytes 393220

commit v2 on v1

v2 whole, which is shorter than its diff:
```python
import functools
import math

import jax
import jax.numpy as jnp
from jax import lax
from jax.experimental import pallas as pl
from jax.experimental.pallas import tpu as pltpu
from jax.sharding import PartitionSpec as P

HEAD_DIM = 128
GROUP = 8
KV_HEADS = 4
TOK = 64
FEAT = 256
HALF = 2048
XC = 256
YC = HALF - XC
PART = YC // 2
PIECES = 2
ROWS = TOK // PIECES
LIMIT = 56
ORDER = ("gy", "rA", "xA", "gA", "T", "o0", "hA", "rB", "xB", "gB", "o1", "hB", "X", "a0", "lA", "lB", "a1", "dw")
EARLY = ("r1", "s1", "cr", "r2", "s2", "cg", "px", "p0", "gY", "p1")
SCALE = 1.0 / math.sqrt(HEAD_DIM)
BF16 = jnp.bfloat16
F32 = jnp.float32
NT = (((1,), (1,)), ((), ()))


def place_of_head(head):
    shard = head // 2
    return (shard // 2) % 4, (shard // 8) * 2 + shard % 2, (head % 2) * HEAD_DIM


def kernel(
    x_ref, kv_ref, w_ref, out_ref, dw_ref,
    q_v, kv_v, w_v, probs, cs, c1, cg, ct, g, gx, sa, op, ra, fwd, bwd, xr, px, rx, xx, xf, xb, dp, dr_part, dr_sib, dr_sec, ds, dc,
    send_sem, load_sem, g_sem, gx_sem, sa_sem, c1_sem, cg_sem, ra_sem, f_sem, b_sem, xr_sem, rx_sem, xx_sem, xf_sem, xb_sem, part_sem, sib_sem, sec_sem, ds_sem, dc_sem,
):
    s = lax.axis_index("section")
    shard = lax.axis_index("shard")
    c = lax.rem(shard, 2)
    y = lax.rem(shard // 2, 4)
    xh = shard // 8
    oc, ox, osec = 1 - c, 1 - xh, 1 - s
    yp, y2, ym = lax.rem(y + 1, 4), lax.rem(y + 2, 4), lax.rem(y + 3, 4)
    y_from, y_to = lax.rem(y + 3 - 2 * xh, 4), lax.rem(y + 1 + 2 * xh, 4)
    first, second = s == 0, s == 1
    own_k = [c, 2 + c]
    other_k = [oc, 2 + oc]
    k_me, k_ox, k_sib = xh * 2 + c, ox * 2 + c, xh * 2 + oc
    near_k = [xh * 2, xh * 2 + 1]
    far_k = [ox * 2, ox * 2 + 1]

    def at(xh_, y_, c_, s_):
        return {"section": s_, "shard": (xh_ * 4 + y_) * 2 + c_}

    sibling = at(xh, y, oc, s)
    up, across, down = at(xh, yp, c, s), at(xh, y2, c, s), at(xh, ym, c, s)
    toward, backward = at(xh, y_to, c, s), at(xh, y_from, c, s)
    row = {(a, b, d): at(a, y, b, d) for a in (0, 1) for b in (0, 1) for d in (0, 1)}
    here = [at(xh, y, c, 0), at(xh, y, c, 1)]
    far = [at(ox, y, c, 0), at(ox, y, c, 1)]
    row_own = [at(a, y, c, 1) for a in (0, 1)]
    near_row = [at(xh, y, b, 0) for b in (0, 1)]
    far_row = [at(ox, y, b, 0) for b in (0, 1)]
    sent = {None: [], 0: [], 1: []}
    count = [0]

    def send(when, src, dst, sem, to):
        slot = count[0]
        count[0] += 1

        def copy():
            return pltpu.make_async_remote_copy(
                src_ref=src(), dst_ref=dst(), send_sem=send_sem.at[slot], recv_sem=sem(),
                device_id=to, device_id_type=pl.DeviceIdType.MESH)

        copy().start()
        sent[when].append(copy)

    def arrive(dst, sem):
        pltpu.make_async_remote_copy(
            src_ref=dst, dst_ref=dst, send_sem=send_sem.at[0], recv_sem=sem,
            device_id=sibling, device_id_type=pl.DeviceIdType.MESH).wait_recv()

    def load(src, dst, i):
        return pltpu.make_async_copy(src, dst, load_sem.at[i])

    load_w = lambda: load(w_ref, w_v, 0)
    load_q = lambda: load(x_ref.at[0], q_v, 1)
    load_kv = lambda: load(kv_ref, kv_v, 2)
    load_own = lambda: load(x_ref.at[0, :, pl.ds(HALF, YC)], g.at[k_me, y], 3)
    load_own_x = lambda: load(x_ref.at[0, :, pl.ds(HALF + YC, XC)], gx.at[k_me, y], 6)

    @pl.when(first)
    def _():
        load_kv().start()
        load_q().start()

    @pl.when(second)
    def _():
        load_own().start()
        load_own_x().start()

    load_w().start()
    barrier = pltpu.get_barrier_semaphore()
    for dx, d_c, d_s in [(dx, d_c, d_s) for d_s in (0, 1) for dx in (0, 1) for d_c in (0, 1)][1:]:
        pl.semaphore_signal(barrier, inc=1, device_id=at(ox if dx else xh, y, oc if d_c else c, osec if d_s else s),
                            device_id_type=pl.DeviceIdType.MESH)
    for other in (up, across, down):
        pl.semaphore_signal(barrier, inc=1, device_id=other, device_id_type=pl.DeviceIdType.MESH)
    pl.semaphore_wait(barrier, 10)

    def piece(k, y_, p):
        return lambda: g.at[k, y_, pl.ds(p * ROWS, ROWS)]

    def piece_sem(k, y_, p):
        return lambda: g_sem.at[k, y_, p]

    def push(when, k, y_, p, to, src=None):
        send(when, src or piece(k, y_, p), piece(k, y_, p), piece_sem(k, y_, p), to)

    def got(k, y_, p):
        arrive(g.at[k, y_, pl.ds(p * ROWS, ROWS)], g_sem.at[k, y_, p])

    def push_x(when, k, y_, to, src=None):
        send(when, src or (lambda: gx.at[k, y_]), lambda: gx.at[k, y_], lambda: gx_sem.at[k, y_], to)

    def push_low(y_, to, src=None):
        send(1, src or (lambda: sa.at[y_]), lambda: sa.at[y_], lambda: sa_sem.at[y_], to)

    def to_first(y_, src=None):
        for to in (here[0], far[0]):
            push_x(1, k_me, y_, to, src or (lambda: sa.at[y_]))

    def low_arrived(y_, to):
        arrive(sa.at[y_], sa_sem.at[y_])
        if to is not None:
            push_low(y_, to)
        to_first(y_)

    def high_arrived(y_, to):
        arrive(gx.at[k_me, y_], gx_sem.at[k_me, y_])
        if to is not None:
            push_x(1, k_me, y_, to)
        push_x(1, k_me, y_, far[1])
        push_x(1, k_me, y_, sibling)

    def far_arrived(y_):
        arrive(gx.at[k_ox, y_], gx_sem.at[k_ox, y_])
        push_x(1, k_ox, y_, sibling)

    def both_arrived(y_):
        for k in (k_me, k_ox):
            arrive(gx.at[k, y_], gx_sem.at[k, y_])
            push_x(0, k, y_, sibling)

    @pl.when(second)
    def _():
        low = [lambda p=p: x_ref.at[0, pl.ds(p * ROWS, ROWS), pl.ds(0, YC)] for p in range(PIECES)]
        high = [lambda p=p: x_ref.at[0, pl.ds(p * ROWS, ROWS), pl.ds(HALF, YC)] for p in range(PIECES)]
        for p in range(PIECES):
            push(1, k_me, y, p, here[0], low[p])
            push(1, k_me, y, p, far[0], low[p])
            push(1, k_me, y, p, up, high[p])
            push(1, k_me, y, p, down, high[p])
        low_x = lambda: x_ref.at[0, :, pl.ds(YC, XC)]
        high_x = lambda: x_ref.at[0, :, pl.ds(HALF + YC, XC)]
        for to in (up, down):
            push_low(y, to, low_x)
            push_x(1, k_me, y, to, high_x)
        to_first(y, low_x)
        for p in range(PIECES):
            push(1, k_me, y, p, far[1], high[p])
            push(1, k_me, y, p, sibling, high[p])
        push_x(1, k_me, y, far[1], high_x)
        push_x(1, k_me, y, sibling, high_x)

    def relay(k, y_, to):
        for p in range(PIECES):
            got(k, y_, p)
            if to is not None:
                push(None, k, y_, p, to)
            push(None, k, y_, p, sibling)

    def row_step(source, y_):
        for a in (0, 1):
            for b in (0, 1):
                send(0, lambda a=a, b=b: source(a * 2 + b), lambda: cg.at[k_me, y_], lambda: cg_sem.at[k_me, y_], row[a, b, 1])
        send(0, lambda: source(k_sib), lambda: cg.at[k_me, y_], lambda: cg_sem.at[k_me, y_], sibling)

    @pl.when(first)
    def _():
        load_kv().wait()
        load_q().wait()
        causal = (lax.rem(lax.broadcasted_iota(jnp.int32, (GROUP * TOK, TOK), 0), TOK)
                  >= lax.broadcasted_iota(jnp.int32, (GROUP * TOK, TOK), 1))
        for h in (0, 2, 1, 3):
            keys = kv_v[0, :, h * HEAD_DIM:(h + 1) * HEAD_DIM]
            values = kv_v[1, :, h * HEAD_DIM:(h + 1) * HEAD_DIM]
            heads = [h * GROUP + i for i in range(GROUP)]
            queries = jnp.concatenate([q_v[:, i * HEAD_DIM:(i + 1) * HEAD_DIM] for i in heads], axis=0)
            scores = lax.dot_general(queries, keys, NT, preferred_element_type=F32) * SCALE
            scores = jnp.where(causal, scores, -1e30)
            shifted = jnp.exp(scores - jnp.max(scores, axis=-1, keepdims=True))
            weights = shifted * (1.0 / jnp.sum(shifted, axis=-1, keepdims=True))
            probs[h] = weights
            mixed = jnp.dot(weights.astype(BF16), values, preferred_element_type=F32).astype(BF16)
            for i, head in enumerate(heads):
                y_, k_, col = place_of_head(head)
                cs[y_, k_, :, col:col + HEAD_DIM] = mixed[i * TOK:(i + 1) * TOK]
        for y_, to in ((yp, up), (ym, down), (y2, across)):
            send(0, lambda y_=y_: cs.at[y_], lambda: c1.at[:, y], lambda: c1_sem.at[y], to)
        row_step(lambda k_: cs.at[y, k_], y)
        cg[k_me, y] = cs[y, k_me]
        for y_ in (yp, ym, y2):
            arrive(c1.at[:, y_], c1_sem.at[y_])
            row_step(lambda k_, y_=y_: c1.at[k_, y_], y_)
            cg[k_me, y_] = c1[k_me, y_]
        for p in range(PIECES):
            for k in (k_me, k_ox):
                got(k, y, p)
                push(0, k, y, p, up)
                push(0, k, y, p, down)
            for k in (k_me, k_ox):
                push(0, k, y, p, sibling)

    def grad(y_):
        for k in other_k:
            for p in range(PIECES):
                got(k, y_, p)
            arrive(gx.at[k, y_], gx_sem.at[k, y_])
        block = g[:, y_].reshape(4 * TOK, YC)
        block_x = gx[:, y_].reshape(4 * TOK, XC)
        value = lax.dot_general(block, w_v[:, :YC], NT, preferred_element_type=F32)
        value += lax.dot_general(block_x, w_v[:, YC:], NT, preferred_element_type=F32)
        dp[y_] = value.reshape(4, TOK, FEAT).astype(BF16)

        @pl.when(first)
        def _():
            send(0, lambda: dp.at[y_, pl.ds(ox * 2, 2)], lambda: dr_part.at[y_], lambda: part_sem.at[y_], here[1])
            send(0, lambda: dp.at[y_, k_sib], lambda: dr_sib.at[y_], lambda: sib_sem.at[y_], sibling)

        @pl.when(second)
        def _():
            for b in (0, 1):
                send(1, lambda b=b: dp.at[y_, near_k[b]], lambda: dr_sec.at[y_, c], lambda: sec_sem.at[y_, c], near_row[b])

    def grad_far(y_):
        @pl.when(second)
        def _():
            arrive(dr_part.at[y_], part_sem.at[y_])
            for b in (0, 1):
                dr_sec[y_, b] = (dp[y_, far_k[b]].astype(F32) + dr_part[y_, b].astype(F32)).astype(BF16)
                send(1, lambda b=b: dr_sec.at[y_, b], lambda: ds.at[y_, k_me], lambda: ds_sem.at[y_, c], far_row[b])

    def grad_along_y(y_, to):
        for b in (0, 1):
            arrive(dr_sec.at[y_, b], sec_sem.at[y_, b])
            arrive(ds.at[y_, far_k[b]], ds_sem.at[y_, b])
        arrive(dr_sib.at[y_], sib_sem.at[y_])
        ds[y_, k_me] = (dp[y_, k_me].astype(F32) + dr_sec[y_, c].astype(F32)).astype(BF16)
        ds[y_, k_sib] = (dr_sib[y_].astype(F32) + dr_sec[y_, oc].astype(F32)).astype(BF16)
        if to is None:
            dc[y] = ds[y_]
        else:
            send(0, lambda: ds.at[y_], lambda: dc.at[y], lambda: dc_sem.at[y], to)

    def product(k, start, size):
        block = cg[k].reshape(4 * TOK, FEAT)
        value = jnp.dot(block, w_v[:, start:start + size], preferred_element_type=F32)
        return value.reshape(4, TOK, size).astype(BF16)

    def partial(k, n):
        op[n, k] = product(k, n * PART, PART)

    def out_x_first():
        for a in (0, 1):
            px[other_k[a]] = product(other_k[a], YC, XC)
            send(None, lambda a=a: px.at[other_k[a]], lambda a=a: rx.at[a], lambda a=a: rx_sem.at[a], sibling)
        for a in (0, 1):
            px[own_k[a]] = product(own_k[a], YC, XC)

        def total_x(a):
            arrive(rx.at[a], rx_sem.at[a])
            px[own_k[a]] = (px[own_k[a]].astype(F32) + rx[a].astype(F32)).astype(BF16)

        for a in (0, 1):
            total_x(a)

        @pl.when(first)
        def _():
            for a in (0, 1):
                send(0, lambda a=a: px.at[own_k[a]], lambda: xx.at[xh], lambda: xx_sem.at[xh], row_own[a])

        @pl.when(second)
        def _():
            send(1, lambda: px.at[k_ox], lambda: xx.at[2], lambda: xx_sem.at[2], far[1])

    def total(n, a, y_, extra):
        arrive(ra.at[n, a, y_], ra_sem.at[n, a, y_])
        k = own_k[a]
        value = op[n, k, y_].astype(F32) + ra[n, a, y_].astype(F32)
        for ref, i in extra:
            value += ref[n, i].astype(F32)
        op[n, k, y_] = value.astype(BF16)

    def pass_on(n, a, y_, buffer, sems, i, to):
        send(None, lambda: op.at[n, own_k[a], y_], lambda: buffer.at[n, i], lambda: sems.at[n, i], to)

    def out_first(n):
        total(n, 0, y2, [])
        pass_on(n, 0, y2, fwd, f_sem, 0, up)
        total(n, 1, y2, [])
        pass_on(n, 1, y2, bwd, b_sem, 0, down)

    def out_direct(n):
        total(n, 1, yp, [])
        pass_on(n, 1, yp, fwd, f_sem, 1, up)
        total(n, 0, ym, [])
        pass_on(n, 0, ym, bwd, b_sem, 1, down)

    def out_relay(n):
        arrive(fwd.at[n, 0], f_sem.at[n, 0])
        total(n, 0, yp, [(fwd, 0)])
        pass_on(n, 0, yp, fwd, f_sem, 2, up)
        arrive(bwd.at[n, 0], b_sem.at[n, 0])
        total(n, 1, ym, [(bwd, 0)])
        pass_on(n, 1, ym, bwd, b_sem, 2, down)

    def out_along_x(n):
        for i in (1, 2):
            arrive(fwd.at[n, i], f_sem.at[n, i])
            arrive(bwd.at[n, i], b_sem.at[n, i])
        total(n, 0, y, [(fwd, 2), (bwd, 1)])
        total(n, 1, y, [(fwd, 1), (bwd, 2)])

        @pl.when(first)
        def _():
            for a in (0, 1):
                send(0, lambda a=a: op.at[n, own_k[a], y], lambda: xr.at[n, xh], lambda: xr_sem.at[n, xh], row_own[a])

        @pl.when(second)
        def _():
            send(1, lambda: op.at[n, k_ox, y], lambda: xr.at[n, 2], lambda: xr_sem.at[n, 2], far[1])

    load_w().wait()

    @pl.when(second)
    def _():
        load_own().wait()
        load_own_x().wait()

    def out_half(n):
        for a in (0, 1):
            partial(other_k[a], n)
            for y_ in (y2, yp, ym, y):
                send(None, lambda a=a, y_=y_: op.at[n, other_k[a], y_], lambda a=a, y_=y_: ra.at[n, a, y_],
                     lambda a=a, y_=y_: ra_sem.at[n, a, y_], sibling)
        for a in (0, 1):
            partial(own_k[a], n)
        out_first(n)
        out_direct(n)

    def early(name):
        if name == "r1":
            relay(k_me, y_from, toward)
        elif name == "s1":
            @pl.when(second)
            def _():
                low_arrived(ym, up)
                high_arrived(yp, down)
                for p in range(PIECES):
                    got(k_ox, y, p)
                    push(1, k_ox, y, p, up)
                    push(1, k_ox, y, p, down)
                    push(1, k_ox, y, p, sibling)
        elif name == "r2":
            relay(k_ox, y_to, backward)
        elif name == "s2":
            @pl.when(first)
            def _():
                both_arrived(y)

            @pl.when(second)
            def _():
                low_arrived(yp, None)
                high_arrived(ym, None)
                far_arrived(y)
        elif name == "cr":
            @pl.when(second)
            def _():
                for y_ in (y, yp, ym, y2):
                    for k in far_k:
                        arrive(cg.at[k, y_], cg_sem.at[k, y_])
                        send(1, lambda k=k, y_=y_: cg.at[k, y_], lambda k=k, y_=y_: cg.at[k, y_],
                             lambda k=k, y_=y_: cg_sem.at[k, y_], here[0])
        elif name == "gY":
            grad(y)
        elif name == "cg":
            @pl.when(first)
            def _():
                for y_ in (y, yp, ym, y2):
                    for k in (k_sib, far_k[0], far_k[1]):
                        arrive(cg.at[k, y_], cg_sem.at[k, y_])

            @pl.when(second)
            def _():
                for y_ in (y, yp, ym, y2):
                    for k in near_k:
                        arrive(cg.at[k, y_], cg_sem.at[k, y_])
        elif name == "px":
            out_x_first()
        elif name in ("p0", "p1"):
            out_half(int(name[1]))

    for name in EARLY:
        early(name)

    def along_y(i, y_, extra, buffer, sems, slot, to):
        if i == 0:
            value = xx[0, y_].astype(F32) + xx[1, y_].astype(F32)
        else:
            value = xx[2, y_].astype(F32) + px[k_me, y_].astype(F32)
        for ref, at_ in extra:
            value += ref[at_].astype(F32)
        if to is None:
            return value.astype(BF16)
        xx[i, y_] = value.astype(BF16)
        send(1, lambda: xx.at[i, y_], lambda: buffer.at[slot], lambda: sems.at[slot], to)

    def steps(name):
        if name == "rA":
            relay(own_k[1], ym, None)
            relay(own_k[0], yp, None)
        elif name == "xA":
            @pl.when(first)
            def _():
                both_arrived(yp)
                both_arrived(ym)

            @pl.when(second)
            def _():
                low_arrived(y2, None)
                high_arrived(y2, None)
                far_arrived(yp)
                far_arrived(ym)
        elif name == "rB":
            relay(own_k[0], y2, None)
            relay(own_k[1], y2, None)
        elif name == "xB":
            @pl.when(first)
            def _():
                both_arrived(y2)

            @pl.when(second)
            def _():
                far_arrived(y2)
        elif name == "gy":
            grad_far(y)
        elif name == "gA":
            grad(yp)
            grad(ym)
        elif name == "gB":
            grad(y2)
        elif name == "hA":
            grad_far(yp)
            grad_far(ym)
        elif name == "hB":
            grad_far(y2)
        elif name == "lA":
            @pl.when(first)
            def _():
                grad_along_y(yp, up)
                grad_along_y(ym, down)
        elif name == "lB":
            @pl.when(first)
            def _():
                grad_along_y(y2, across)
                grad_along_y(y, None)
        elif name == "T":
            @pl.when(second)
            def _():
                for i in range(3):
                    arrive(xx.at[i], xx_sem.at[i])
                along_y(0, y2, [], xf, xf_sem, 0, up)
                along_y(2, y2, [], xb, xb_sem, 0, down)
                along_y(0, ym, [], xb, xb_sem, 1, down)
                along_y(2, yp, [], xf, xf_sem, 1, up)
        elif name == "X":
            @pl.when(second)
            def _():
                arrive(xf.at[0], xf_sem.at[0])
                along_y(0, yp, [(xf, 0)], xf, xf_sem, 2, up)
                arrive(xb.at[0], xb_sem.at[0])
                along_y(2, ym, [(xb, 0)], xb, xb_sem, 2, down)
        elif name in ("o0", "o1"):
            out_relay(int(name[1]))
        elif name in ("a0", "a1"):
            out_along_x(int(name[1]))
        elif name == "dw":
            ct[...] = cg[...].reshape(16 * TOK, FEAT).T
            weight_grad(g, YC, 0)
            weight_grad(gx, XC, YC)

    def weight_grad(source, size, start):
        @pl.loop(0, size // FEAT)
        def _(n):
            cols = pl.ds(pl.multiple_of(n * FEAT, FEAT), FEAT)
            place = pl.ds(pl.multiple_of(start + n * FEAT, FEAT), FEAT)
            block = source[:, :, :, cols].reshape(16 * TOK, FEAT)
            dw_ref[:, place] = jnp.dot(ct[...], block, preferred_element_type=F32).astype(BF16)

    for name in ORDER:
        steps(name)

    @pl.when(first)
    def _():
        for y_ in (yp, ym, y2):
            arrive(dc.at[y_], dc_sem.at[y_])
        for h in range(KV_HEADS):
            keys = kv_v[0, :, h * HEAD_DIM:(h + 1) * HEAD_DIM]
            values = kv_v[1, :, h * HEAD_DIM:(h + 1) * HEAD_DIM]
            heads = [h * GROUP + i for i in range(GROUP)]
            parts = []
            for head in heads:
                y_, k_, col = place_of_head(head)
                parts.append(dc[y_, k_, :, col:col + HEAD_DIM])
            grads = jnp.concatenate(parts, axis=0)
            grad_probs = lax.dot_general(grads, values, NT, preferred_element_type=F32)
            weights = probs[h]
            mean = jnp.sum(weights * grad_probs, axis=-1, keepdims=True)
            grad_scores = (weights * (grad_probs - mean) * SCALE).astype(BF16)
            grad_queries = jnp.dot(grad_scores, keys, preferred_element_type=F32).astype(BF16)
            for i, head in enumerate(heads):
                out_ref[0, :, head * HEAD_DIM:(head + 1) * HEAD_DIM] = grad_queries[i * TOK:(i + 1) * TOK]

    @pl.when(second)
    def _():
        for i in (1, 2):
            arrive(xf.at[i], xf_sem.at[i])
            arrive(xb.at[i], xb_sem.at[i])
        out_ref[0, :, YC:HALF] = along_y(0, y, [(xf, 2), (xb, 1)], None, None, None, None)
        out_ref[0, :, HALF + YC:] = along_y(2, y, [(xf, 1), (xb, 2)], None, None, None, None)
        for n in (0, 1):
            for i in range(3):
                arrive(xr.at[n, i], xr_sem.at[n, i])
            out_ref[0, :, n * PART:(n + 1) * PART] = (xr[n, 0].astype(F32) + xr[n, 1].astype(F32)).astype(BF16)
            out_ref[0, :, HALF + n * PART:HALF + (n + 1) * PART] = (xr[n, 2].astype(F32) + op[n, k_me, y].astype(F32)).astype(BF16)


    for copy in sent[None]:
        copy().wait_send()
    for which in (0, 1):
        @pl.when(s == which)
        def _():
            for copy in sent[which]:
                copy().wait_send()


def body(section_inputs, keys_values, out_weight):
    dma = pltpu.SemaphoreType.DMA
    scratch = [
        pltpu.VMEM((TOK, 4096), BF16),
        pltpu.VMEM((2, TOK, 512), BF16),
        pltpu.VMEM((FEAT, HALF), BF16),
        pltpu.VMEM((KV_HEADS, GROUP * TOK, TOK), F32),
        pltpu.VMEM((4, 4, TOK, FEAT), BF16),
        pltpu.VMEM((4, 4, TOK, FEAT), BF16),
        pltpu.VMEM((4, 4, TOK, FEAT), BF16),
        pltpu.VMEM((FEAT, 16 * TOK), BF16),
        pltpu.VMEM((4, 4, TOK, YC), BF16),
        pltpu.VMEM((4, 4, TOK, XC), BF16),
        pltpu.VMEM((4, TOK, XC), BF16),
        pltpu.VMEM((2, 4, 4, TOK, PART), BF16),
        pltpu.VMEM((2, 2, 4, TOK, PART), BF16),
        pltpu.VMEM((2, 3, TOK, PART), BF16),
        pltpu.VMEM((2, 3, TOK, PART), BF16),
        pltpu.VMEM((2, 3, TOK, PART), BF16),
        pltpu.VMEM((4, 4, TOK, XC), BF16),
        pltpu.VMEM((2, 4, TOK, XC), BF16),
        pltpu.VMEM((3, 4, TOK, XC), BF16),
        pltpu.VMEM((3, TOK, XC), BF16),
        pltpu.VMEM((3, TOK, XC), BF16),
        pltpu.VMEM((4, 4, TOK, FEAT), BF16),
        pltpu.VMEM((4, 2, TOK, FEAT), BF16),
        pltpu.VMEM((4, TOK, FEAT), BF16),
        pltpu.VMEM((4, 2, TOK, FEAT), BF16),
        pltpu.VMEM((4, 4, TOK, FEAT), BF16),
        pltpu.VMEM((4, 4, TOK, FEAT), BF16),
        dma((256,)), dma((7,)), dma((4, 4, PIECES)), dma((4, 4)), dma((4,)), dma((4,)), dma((4, 4)), dma((2, 2, 4)), dma((2, 3)), dma((2, 3)), dma((2, 3)),
        dma((2,)), dma((3,)), dma((3,)), dma((3,)),
        dma((4,)), dma((4,)), dma((4, 2)), dma((4, 2)), dma((4,)),
    ]
    anywhere = pl.BlockSpec(memory_space=pl.ANY)
    return pl.pallas_call(
        kernel,
        out_shape=(pltpu.VMEM(section_inputs.shape, BF16), pltpu.VMEM(out_weight.shape, BF16)),
        in_specs=[anywhere] * 3,
        out_specs=(pl.BlockSpec(memory_space=pltpu.VMEM), pl.BlockSpec(memory_space=pltpu.VMEM)),
        scratch_shapes=scratch,
        compiler_params=pltpu.CompilerParams(
            collective_id=0, has_side_effects=True, vmem_limit_bytes=LIMIT * 1024 * 1024),
        cost_estimate=pl.CostEstimate(flops=3 * 2 * 1024 * 256 * 2048, bytes_accessed=4 << 20, transcendentals=1 << 17),
    )(section_inputs, keys_values, out_weight)


def solution(mesh):
    placed = (
        P("section", ("pair", "shard"), None),
        P(None, ("pair", "shard"), None),
        P("shard", "section"),
    )
    return jax.shard_map(
        body,
        mesh=mesh,
        in_specs=placed,
        out_specs=(P("section", ("pair", "shard"), None), P(("pair", "shard"), "section")),
        check_vma=False,
    )
```

time: 72.5 us -> 65 us (0.90)
  the two profiles are of different devices: /device:TPU:23 before, /device:TPU:3 now
where the time goes in v2:
time: 65 us; the launch traced here: 64.8 us
  Pallas kernels  62.4 us (96%)
  local copies, waits for them, and re-layouts  1.77 us (3%)
    pallas_call x1, Pallas kernels, body(): pl.pallas_call(kernel, out_shape=(pltpu.VMEM(section_inputs.shape, BF16),...  62.4 us
    unnamed x2, local copies, waits for them, and re-layouts  1.77 us

profile of v2, /device:TPU:3, one launch (start us, length us, event | category | flops | bytes accessed | tf_op | source)
XLA Modules:
  0.0 64.8 jit_solution(14555067811129103851)
XLA Ops:
  0.6 62.4 %shard_map.50 = (bf16[1,64,4096]{2,1,0:T(8,128)(2,1)S(1)}, bf16[256,2048]{1,0:T(8,128)(2,1)S(1)}) custom-call(bf16[1,64,4096]{2,1,0:T(8,128)(2,1)} %x_ref.1, bf16[2,64,512]{2,1,0:T(8,128)(2,1)} %kv_ref.1, bf16[256,2048]{1,0:T(8,128)(2,1)} %w_ref.1), custom_call_target="tpu_custom_call" | custom-call | flops 3221225472 | bytes 4194304 | tf_op jit(solution)/shard_map/pallas_call | solution.py:598
  63.1 0.8 %copy.7 = bf16[1,64,4096]{2,1,0:T(8,128)(2,1)} copy(bf16[1,64,4096]{2,1,0:T(8,128)(2,1)S(1)} %get-tuple-element.2) | data formatting | bytes 1048576
  63.9 1.0 %copy.8 = bf16[256,2048]{1,0:T(8,128)(2,1)} copy(bf16[256,2048]{1,0:T(8,128)(2,1)S(1)} %get-tuple-element.3) | data formatting | bytes 2097152

commit v3 on v2

--- a/solution.py
+++ b/solution.py
@@ -17,10 +17,10 @@
 XC = 256
 YC = HALF - XC
 PART = YC // 2
-PIECES = 2
+PIECES = 4
 ROWS = TOK // PIECES
 LIMIT = 56
-ORDER = ("gy", "rA", "xA", "gA", "T", "o0", "hA", "rB", "xB", "gB", "o1", "hB", "X", "a0", "lA", "lB", "a1", "dw")
+ORDER = ("gy", "rA", "xA", "gA", "hA", "T", "o0", "rB", "xB", "gB", "o1", "X", "hB", "a0", "lA", "lB", "a1", "dw")
 EARLY = ("r1", "s1", "cr", "r2", "s2", "cg", "px", "p0", "gY", "p1")
 SCALE = 1.0 / math.sqrt(HEAD_DIM)
 BF16 = jnp.bfloat16

time: 65 us -> 64.2 us (0.988)
  Pallas kernels: 62.4 us -> 61.7 us
    pallas_call x1, Pallas kernels: 62.4 us -> 61.7 us  [body(): pl.pallas_call(kernel, out_shape=(pltpu.VMEM(section_inputs.shape, BF16),...]
where the time goes in v3:
time: 64.2 us; the launch traced here: 64.1 us
  Pallas kernels  61.7 us (96%)
  local copies, waits for them, and re-layouts  1.77 us (3%)
    pallas_call x1, Pallas kernels, body(): pl.pallas_call(kernel, out_shape=(pltpu.VMEM(section_inputs.shape, BF16),...  61.7 us
    unnamed x2, local copies, waits for them, and re-layouts  1.77 us

profile of v3, /device:TPU:3, one launch (start us, length us, event | category | flops | bytes accessed | tf_op | source)
XLA Modules:
  0.0 64.1 jit_solution(4445230687658605096)
XLA Ops:
  0.6 61.7 %shard_map.50 = (bf16[1,64,4096]{2,1,0:T(8,128)(2,1)S(1)}, bf16[256,2048]{1,0:T(8,128)(2,1)S(1)}) custom-call(bf16[1,64,4096]{2,1,0:T(8,128)(2,1)} %x_ref.1, bf16[2,64,512]{2,1,0:T(8,128)(2,1)} %kv_ref.1, bf16[256,2048]{1,0:T(8,128)(2,1)} %w_ref.1), custom_call_target="tpu_custom_call" | custom-call | flops 3221225472 | bytes 4194304 | tf_op jit(solution)/shard_map/pallas_call | solution.py:598
  62.3 0.8 %copy.7 = bf16[1,64,4096]{2,1,0:T(8,128)(2,1)} copy(bf16[1,64,4096]{2,1,0:T(8,128)(2,1)S(1)} %get-tuple-element.2) | data formatting | bytes 1048576
  63.1 1.0 %copy.8 = bf16[256,2048]{1,0:T(8,128)(2,1)} copy(bf16[256,2048]{1,0:T(8,128)(2,1)S(1)} %get-tuple-element.3) | data formatting | bytes 2097152

commit v4 on v3

--- a/solution.py
+++ b/solution.py
@@ -15,13 +15,14 @@
 FEAT = 256
 HALF = 2048
 XC = 256
+CFIRST = True
 YC = HALF - XC
 PART = YC // 2
 PIECES = 4
 ROWS = TOK // PIECES
 LIMIT = 56
 ORDER = ("gy", "rA", "xA", "gA", "hA", "T", "o0", "rB", "xB", "gB", "o1", "X", "hB", "a0", "lA", "lB", "a1", "dw")
-EARLY = ("r1", "s1", "cr", "r2", "s2", "cg", "px", "p0", "gY", "p1")
+EARLY = ("r1", "s1", "cr", "r2", "s2", "px", "p0", "gY", "p1")
 SCALE = 1.0 / math.sqrt(HEAD_DIM)
 BF16 = jnp.bfloat16
 F32 = jnp.float32
@@ -215,17 +216,20 @@
             send(0, lambda y_=y_: cs.at[y_], lambda: c1.at[:, y], lambda: c1_sem.at[y], to)
         row_step(lambda k_: cs.at[y, k_], y)
         cg[k_me, y] = cs[y, k_me]
-        for y_ in (yp, ym, y2):
-            arrive(c1.at[:, y_], c1_sem.at[y_])
-            row_step(lambda k_, y_=y_: c1.at[k_, y_], y_)
-            cg[k_me, y_] = c1[k_me, y_]
-        for p in range(PIECES):
-            for k in (k_me, k_ox):
-                got(k, y, p)
-                push(0, k, y, p, up)
-                push(0, k, y, p, down)
-            for k in (k_me, k_ox):
-                push(0, k, y, p, sibling)
+        def one():
+            for y_ in (yp, ym, y2):
+                arrive(c1.at[:, y_], c1_sem.at[y_])
+                row_step(lambda k_, y_=y_: c1.at[k_, y_], y_)
+                cg[k_me, y_] = c1[k_me, y_]
+        def two():
+            for p in range(PIECES):
+                for k in (k_me, k_ox):
+                    got(k, y, p)
+                    push(0, k, y, p, up)
+                    push(0, k, y, p, down)
+                for k in (k_me, k_ox):
+                    push(0, k, y, p, sibling)
+        for z in ((one, two) if CFIRST else (two, one)): z()
 
     def grad(y_):
         for k in other_k:
@@ -276,11 +280,23 @@
     def partial(k, n):
         op[n, k] = product(k, n * PART, PART)
 
+    def block_ready(k, a, other):
+        def wait():
+            for y_ in (y, yp, ym, y2):
+                arrive(cg.at[k, y_], cg_sem.at[k, y_])
+
+        if other:
+            pl.when(jnp.logical_or(first, xh == a))(wait)
+        else:
+            pl.when(jnp.logical_or(jnp.logical_and(first, xh != a), jnp.logical_and(second, xh == a)))(wait)
+
     def out_x_first():
         for a in (0, 1):
+            block_ready(other_k[a], a, True)
             px[other_k[a]] = product(other_k[a], YC, XC)
             send(None, lambda a=a: px.at[other_k[a]], lambda a=a: rx.at[a], lambda a=a: rx_sem.at[a], sibling)
         for a in (0, 1):
+            block_ready(own_k[a], a, False)
             px[own_k[a]] = product(own_k[a], YC, XC)
 
         def total_x(a):
@@ -399,25 +415,10 @@
                              lambda k=k, y_=y_: cg_sem.at[k, y_], here[0])
         elif name == "gY":
             grad(y)
-        elif name == "cg":
-            @pl.when(first)
-            def _():
-                for y_ in (y, yp, ym, y2):
-                    for k in (k_sib, far_k[0], far_k[1]):
-                        arrive(cg.at[k, y_], cg_sem.at[k, y_])
-
-            @pl.when(second)
-            def _():
-                for y_ in (y, yp, ym, y2):
-                    for k in near_k:
-                        arrive(cg.at[k, y_], cg_sem.at[k, y_])
         elif name == "px":
             out_x_first()
         elif name in ("p0", "p1"):
             out_half(int(name[1]))
-
-    for name in EARLY:
-        early(name)
 
     def along_y(i, y_, extra, buffer, sems, slot, to):
         if i == 0:
@@ -513,7 +514,8 @@
             block = source[:, :, :, cols].reshape(16 * TOK, FEAT)
             dw_ref[:, place] = jnp.dot(ct[...], block, preferred_element_type=F32).astype(BF16)
 
-    for name in ORDER:
+    for name in EARLY + ORDER:
+        early(name)
         steps(name)
 
     @pl.when(first)

time: 64.2 us -> 64.3 us (level)
  no operation moved by 1% of the time
where the time goes in v4:
time: 64.3 us; the launch traced here: 64.2 us
  Pallas kernels  61.8 us (96%)
  local copies, waits for them, and re-layouts  1.77 us (3%)
    pallas_call x1, Pallas kernels, body(): pl.pallas_call(kernel, out_shape=(pltpu.VMEM(section_inputs.shape, BF16),...  61.8 us
    unnamed x2, local copies, waits for them, and re-layouts  1.77 us

profile of v4, /device:TPU:3, one launch (start us, length us, event | category | flops | bytes accessed | tf_op | source)
XLA Modules:
  0.0 64.2 jit_solution(4765117343383320969)
XLA Ops:
  0.6 61.8 %shard_map.50 = (bf16[1,64,4096]{2,1,0:T(8,128)(2,1)S(1)}, bf16[256,2048]{1,0:T(8,128)(2,1)S(1)}) custom-call(bf16[1,64,4096]{2,1,0:T(8,128)(2,1)} %x_ref.1, bf16[2,64,512]{2,1,0:T(8,128)(2,1)} %kv_ref.1, bf16[256,2048]{1,0:T(8,128)(2,1)} %w_ref.1), custom_call_target="tpu_custom_call" | custom-call | flops 3221225472 | bytes 4194304 | tf_op jit(solution)/shard_map/pallas_call | solution.py:600
  62.4 0.8 %copy.7 = bf16[1,64,4096]{2,1,0:T(8,128)(2,1)} copy(bf16[1,64,4096]{2,1,0:T(8,128)(2,1)S(1)} %get-tuple-element.2) | data formatting | bytes 1048576
  63.2 1.0 %copy.8 = bf16[256,2048]{1,0:T(8,128)(2,1)} copy(bf16[256,2048]{1,0:T(8,128)(2,1)S(1)} %get-tuple-element.3) | data formatting | bytes 2097152
